TPU v7x, 32 devices: a whole 2x2x4 slice. The times are simulated.
32 devices in a mesh: ctx: 16 (over z, x, core), head: 2 (over y).
Axes of the slice: x: 2, y: 2, z: 4, core: 2. Of those that a mesh axis runs over, the one named last changes fastest.
Arguments:
- queries: bfloat16 [6144, 64, 128], P(('ctx', 'head')), may hold values from -6 to 6
- keys: bfloat16 [6144, 64, 128], P(('ctx', 'head')), may hold values from -6 to 6
- values: bfloat16 [6144, 64, 128], P(('ctx', 'head')), may hold values from -6 to 6
- decay_log: bfloat16 [6144, 64], P(('ctx', 'head')), may hold values from -1 to 0, as said below
- out_gain: float32 [64, 128], replicated, may hold values from 0.1 to 1.9
Outputs:
- normed: bfloat16 [6144, 64, 128], P(('ctx', 'head'))
Inputs may be any that keep to these rules, and one draw needn't show every extreme that they name: `decay_log`: every entry is negative or zero.
All inputs are finite; a program needn't handle non-finite values.
Results may differ from a plain program's by a relative error of at most 0.01.
Values may be sent and summed in bfloat16 or wider, within the bound.
A program may use at most 128 MiB of HBM per device.

v0:
```python
import jax
import jax.numpy as jnp
from jax import lax
from jax.sharding import PartitionSpec as P


def prefix_2(part, axis, combine, identity):
    place = lax.axis_index(axis)
    gathered = jax.tree.map(lambda a: lax.all_gather(a, axis), part)
    state = jax.tree.map(lambda a, e: jnp.zeros_like(a) + jnp.asarray(e, a.dtype), part, identity)

    def one(step, state):
        return combine(
            state, jax.tree.map(lambda a: lax.dynamic_index_in_dim(a, step, 0, False), gathered)
        )

    return lax.fori_loop(0, place, one, state)


def activate(block):
    return jax.nn.silu(block.astype(jnp.float32)).astype(jnp.bfloat16)


def join_states(earlier, later):
    return (earlier[0] + later[0], jnp.exp(later[0])[:, None, None] * earlier[1] + later[1])


def empty_pair(pair):
    return (jnp.zeros_like(pair[0]), jnp.zeros_like(pair[1]))


def prefix_whole(pair):
    return prefix_2(pair, "ctx", join_states, empty_pair(pair))


def attend(pieces, prefix):
    queries_x, keys_x, values_x, decay_x = pieces
    query_act = activate(queries_x[:, 0])
    key_act = activate(keys_x[:, 0])
    value_act = activate(values_x[:, 0])
    decays = decay_x[:, 0].astype(jnp.float32)
    length = query_act.shape[0]
    token_position_index = lax.iota(jnp.int32, length)
    causal = token_position_index[:, None] >= token_position_index[None, :]
    lower_tri = causal.astype(jnp.float32)
    cumulative = jnp.dot(lower_tri, decays, precision=lax.Precision.HIGHEST)
    scores = jnp.einsum("thd,shd->hts", query_act, key_act, preferred_element_type=jnp.float32)
    offsets = cumulative.T[:, :, None] - cumulative.T[:, None, :]
    causal_heads = causal[None]
    weights = jnp.where(
        causal_heads, scores * jnp.exp(jnp.where(causal_heads, offsets, -1e30)), 0.0
    )
    weights = weights.astype(jnp.bfloat16)
    intra_out = jnp.einsum("hts,shd->thd", weights, value_act, preferred_element_type=jnp.float32)
    ending = cumulative[-1]
    scaled_keys = (
        key_act.astype(jnp.float32) * jnp.exp(ending[None, :] - cumulative)[:, :, None]
    ).astype(jnp.bfloat16)
    local_state = jnp.einsum(
        "shd,she->hde", scaled_keys, value_act, preferred_element_type=jnp.float32
    )
    incoming = prefix((ending, local_state))[1]
    inter_out = jnp.einsum(
        "thd,hde->the", query_act, incoming.astype(jnp.bfloat16), preferred_element_type=jnp.float32
    )
    inter_out = inter_out * jnp.exp(cumulative)[:, :, None]
    return (intra_out + inter_out).astype(jnp.bfloat16)[:, None]


def normalize(mixed, out_gain):
    values32 = mixed.astype(jnp.float32)
    meansq = jnp.mean(values32 * values32, axis=(1, 2), keepdims=True)
    return (values32 * lax.rsqrt(meansq + 1e-06) * out_gain[None]).astype(jnp.bfloat16)


def shards(queries, keys, values, decay_log, out_gain):
    row_count, heads, head_dim = queries.shape
    groups = lax.axis_size("head")
    per_group = heads // groups
    queries_g = queries.reshape(row_count, groups, per_group, head_dim)
    keys_g = keys.reshape(row_count, groups, per_group, head_dim)
    values_g = values.reshape(row_count, groups, per_group, head_dim)
    decay_g = decay_log.reshape(row_count, groups, per_group)
    pieces = (
        lax.all_to_all(queries_g, "head", split_axis=1, concat_axis=0, tiled=True),
        lax.all_to_all(keys_g, "head", split_axis=1, concat_axis=0, tiled=True),
        lax.all_to_all(values_g, "head", split_axis=1, concat_axis=0, tiled=True),
        lax.all_to_all(decay_g, "head", split_axis=1, concat_axis=0, tiled=True),
    )
    attended = attend(pieces, prefix_whole)
    returned = lax.all_to_all(attended, "head", split_axis=0, concat_axis=1, tiled=True)
    mixed = returned.reshape(row_count, heads, head_dim)
    return normalize(mixed, out_gain)


def solution(mesh):
    return jax.shard_map(
        shards,
        mesh=mesh,
        in_specs=(
            P(("ctx", "head"), None, None),
            P(("ctx", "head"), None, None),
            P(("ctx", "head"), None, None),
            P(("ctx", "head"), None),
            P(),
        ),
        out_specs=P(("ctx", "head"), None, None),
        check_vma=False,
    )
```

profile of v0, /device:TPU:27, one launch (start us, length us, event | category | flops | bytes accessed | tf_op | source)
XLA Modules:
  0.0 403.6 jit_solution(17422104793808244292)
XLA Ops:
  6.5 3.3 all-to-all-start.3
  9.8 4.1 %copy.65 = bf16[192,2,32,128]{3,2,0,1:T(8,128)(2,1)} copy(bf16[192,2,32,128]{3,2,1,0:T(8,128)(2,1)} %bitcast.71) | data formatting | bytes 6291456 | tf_op jit(solution)/shard_map/reshape | solution.py:81
  13.9 3.9 all-to-all-start.2
  17.9 4.1 %copy.59 = bf16[192,2,32,128]{3,2,0,1:T(8,128)(2,1)} copy(bf16[192,2,32,128]{3,2,1,0:T(8,128)(2,1)} %bitcast.72) | data formatting | bytes 6291456 | tf_op jit(solution)/shard_map/reshape | solution.py:82
  22.0 31.3 %all-to-all-done.2 = bf16[192,2,32,128]{3,2,0,1:T(8,128)(2,1)S(1)} async-done(((bf16[192,2,32,128]{3,2,0,1:T(8,128)(2,1)}), bf16[192,2,32,128]{3,2,0,1:T(8,128)(2,1)S(1)}, u32[]{:S(2)}, u32[]{:S(2)}) %all-to-all-start.2) | async-done | bytes 3145760 | tf_op jit(solution)/shard_map/all_to_all | solution.py:86
  53.3 5.2 %all-to-all-start = ((bf16[192,2,32,128]{3,2,0,1:T(8,128)(2,1)}), bf16[192,2,32,128]{3,2,0,1:T(8,128)(2,1)}, u32[]{:S(2)}, u32[]{:S(2)}) async-start(bf16[192,2,32,128]{3,2,0,1:T(8,128)(2,1)} %copy.59), calls=%async_computation | async-start | bytes 6291456 | tf_op jit(solution)/shard_map/all_to_all | solution.py:87
  59.2 3.5 bitcast_convert_fusion.1
  62.7 30.5 %all-to-all-done = bf16[192,2,32,128]{3,2,0,1:T(8,128)(2,1)} async-done(((bf16[192,2,32,128]{3,2,0,1:T(8,128)(2,1)}), bf16[192,2,32,128]{3,2,0,1:T(8,128)(2,1)}, u32[]{:S(2)}, u32[]{:S(2)}) %all-to-all-start) | async-done | bytes 3145760 | tf_op jit(solution)/shard_map/all_to_all | solution.py:87
  93.2 2.9 bitcast_convert_fusion.3
  96.1 2.6 copy-done.1
  98.7 16.5 %fusion.10 = f32[32,128,128]{2,1,0:T(8,128)} fusion(f32[384,32]{0,1:T(8,128)S(1)} %get-tuple-element.61, f32[384,32,128]{2,1,0:T(8,128)S(1)} %bitcast.66, f32[384,32,128]{2,1,0:T(8,128)S(1)} %bitcast.65), kind=kOutput, calls=%fused_computation.19 | convolution fusion | flops 423100416 | bytes 14729216 | tf_op jit(solution)/shard_map/shd,she->hde/dot_general | solution.py:59
  115.2 2.2 copy.62
  117.4 3.9 all-to-all-start.1
  121.4 18.6 %all-gather.1 = f32[16,1,32]{2,1,0:T(1,128)S(1)} all-gather(f32[1,1,32]{2,1,0:T(1,128)S(1)} %bitcast.78), channel_id=1, replica_groups=mesh['ctx'=16,'head'=2] {'ctx'}, dimensions={0}, use_global_device_ids=true | all-gather | bytes 2176 | tf_op jit(solution)/shard_map/all_gather | solution.py:9
  140.0 15.1 %all-to-all-done.1 = bf16[192,2,32,128]{3,2,0,1:T(8,128)(2,1)S(1)} async-done(((bf16[192,2,32,128]{3,2,0,1:T(8,128)(2,1)}), bf16[192,2,32,128]{3,2,0,1:T(8,128)(2,1)S(1)}, u32[]{:S(2)}, u32[]{:S(2)}) %all-to-all-start.1) | async-done | bytes 3145760 | tf_op jit(solution)/shard_map/all_to_all | solution.py:85
  155.1 3.5 bitcast_convert_fusion.2
  158.6 126.2 %all-gather.4.cloned.1.call-done = f32[512,128,128]{2,1,0:T(8,128)} async-done(((f32[32,128,128]{2,1,0:T(8,128)}), f32[512,128,128]{2,1,0:T(8,128)}) %all-gather.4.cloned.1.call-update) | async-done | bytes 33554448 | tf_op jit(solution)/shard_map/all_gather | solution.py:9
  285.0 30.6 %while.12 = (s32[]{:T(128)}, f32[32,128,128]{2,1,0:T(8,128)S(1)}, s32[]{:T(128)}, f32[16,32]{1,0:T(8,128)S(1)}, f32[16,32,128,128]{3,2,1,0:T(8,128)}, /*index=5*/s32[]{:T(128)}, s32[]{:T(128)}, s32[]{:T(128)}) while((s32[]{:T(128)}, f32[32,128,128]{2,1,0:T(8,128)S(1)}, s32[]{:T(128)}, f32[16,32]{1,0:T(8,128)S(1)}, ...), condition=%wide.region_1.2_spmd, body=%wide.region_0.1_spmd.sunk | while | flops 1048581 | bytes 6291967 | solution.py:17
  285.0 2.0 bitcast_add_fusion.2
  287.1 2.0 bitcast_add_fusion.2
  289.1 2.0 bitcast_add_fusion.2
  291.1 2.0 bitcast_add_fusion.2
  293.1 2.0 bitcast_add_fusion.2
  295.2 2.0 bitcast_add_fusion.2
  297.2 2.0 bitcast_add_fusion.2
  307.3 2.0 bitcast_add_fusion.2
  315.6 12.1 %fusion.13 = f32[32,128,384]{2,1,0:T(8,128)} fusion(f32[32,128,128]{2,1,0:T(8,128)S(1)} %get-tuple-element.49, f32[384,32,128]{2,1,0:T(8,128)} %bitcast.68), kind=kOutput, calls=%fused_computation.26 | convolution fusion | flops 411041792 | bytes 14680064 | tf_op jit(solution)/shard_map/thd,hde->the/dot_general | solution.py:63
  327.7 16.4 %fusion.11 = bf16[384,1,32,128]{0,3,2,1:T(8,128)(2,1)} fusion(f32[32,128,384]{2,1,0:T(8,128)} %fusion.13, f32[384,32]{0,1:T(8,128)S(1)} %get-tuple-element.60, f32[32,384]{1,0:T(8,128)S(1)} %bitcast.75, pred[384,384]{1,0:T(8,128)(4,1)S(1)} %iota_compare_fusion, f32[384,32,128]{2,1,0:T(8,128)} %bitcast.69, f32[384,32,128]{2,1,0:T(8,128)} %bitcast.67, ...), kind=kOutput, calls=%fused_computation.20 | convolution fusion | flops 2467823616 | bytes 28557312 | tf_op jit(solution)/shard_map/hts,shd->thd/dot_general | solution.py:54
  344.1 4.1 %copy.72 = bf16[384,1,32,128]{3,2,1,0:T(8,128)(2,1)S(1)} copy(bf16[384,1,32,128]{0,3,2,1:T(8,128)(2,1)} %fusion.11) | data formatting | bytes 6291456 | tf_op jit(solution)/shard_map/broadcast_in_dim | solution.py:67
  348.1 37.7 %all_to_all.51 = bf16[384,1,32,128]{3,2,1,0:T(8,128)(2,1)S(1)} all-to-all(bf16[384,1,32,128]{3,2,1,0:T(8,128)(2,1)S(1)} %copy.72), channel_id=1, replica_groups=mesh['ctx'=16,'head'=2] {'head'}, dimensions={0} | all-to-all | bytes 6291456 | tf_op jit(solution)/shard_map/all_to_all | solution.py:91
  386.7 3.4 copy.74
  391.6 5.2 %multiply_convert_fusion = bf16[192,64,128]{2,1,0:T(8,128)(2,1)} fusion(f32[192,64,128]{2,1,0:T(8,128)} %bitcast.62, f32[64,128]{1,0:T(8,128)S(1)} %copy-done.3, f32[192]{0:T(256)S(1)} %add_rsqrt_fusion), kind=kLoop, calls=%fused_computation.13 | loop fusion | flops 4718592 | bytes 9470720 | tf_op jit(solution)/shard_map/convert_element_type | solution.py:73
  (44 shorter events, 17.3 us)
Async XLA Ops:
  6.5 7.4 %all-to-all-start.3 = ((bf16[192,2,32]{0,2,1:T(8,128)(2,1)}), bf16[192,2,32]{0,2,1:T(8,128)(2,1)S(1)}, u32[]{:S(2)}, u32[]{:S(2)}) async-start(bf16[192,2,32]{0,2,1:T(8,128)(2,1)} %bitcast.76), calls=%async_computation.3 | async-start | bytes 65536 | tf_op jit(solution)/shard_map/all_to_all | solution.py:88
  13.9 39.4 %all-to-all-start.2 = ((bf16[192,2,32,128]{3,2,0,1:T(8,128)(2,1)}), bf16[192,2,32,128]{3,2,0,1:T(8,128)(2,1)S(1)}, u32[]{:S(2)}, u32[]{:S(2)}) async-start(bf16[192,2,32,128]{3,2,0,1:T(8,128)(2,1)} %copy.65), calls=%async_computation.2 | async-start | bytes 6291456 | tf_op jit(solution)/shard_map/all_to_all | solution.py:86
  53.3 39.8 %all-to-all-start = ((bf16[192,2,32,128]{3,2,0,1:T(8,128)(2,1)}), bf16[192,2,32,128]{3,2,0,1:T(8,128)(2,1)}, u32[]{:S(2)}, u32[]{:S(2)}) async-start(bf16[192,2,32,128]{3,2,0,1:T(8,128)(2,1)} %copy.59), calls=%async_computation | async-start | bytes 6291456 | tf_op jit(solution)/shard_map/all_to_all | solution.py:87
  58.5 226.2 %all-gather.4.cloned.1.call-start = ((), (), s32[]{:S(2)}) async-start(), calls=%async_computation.5 | async-start | bytes 35651584 | tf_op jit(solution)/shard_map/all_gather | solution.py:9
  93.2 5.5 %copy-start = (f32[192,2,1,32,128]{4,3,0,1,2:T(8,128)S(1)}, f32[192,2,1,32,128]{4,3,0,1,2:T(8,128)}, u32[]{:S(2)}) copy-start(f32[192,2,1,32,128]{4,3,0,1,2:T(8,128)} %bitcast_convert_fusion.1) | copy-start | bytes 18874372
  96.1 2.6 copy-start.1
  98.7 16.5 %copy-start.2 = (bf16[192,64,128]{2,1,0:T(8,128)(2,1)S(1)}, bf16[192,64,128]{2,1,0:T(8,128)(2,1)}, u32[]{:S(2)}) copy-start(bf16[192,64,128]{2,1,0:T(8,128)(2,1)} %param.7) | copy-start | bytes 9437188
  117.4 37.7 %all-to-all-start.1 = ((bf16[192,2,32,128]{3,2,0,1:T(8,128)(2,1)}), bf16[192,2,32,128]{3,2,0,1:T(8,128)(2,1)S(1)}, u32[]{:S(2)}, u32[]{:S(2)}) async-start(bf16[192,2,32,128]{3,2,0,1:T(8,128)(2,1)} %copy.62), calls=%async_computation.1 | async-start | bytes 6291456 | tf_op jit(solution)/shard_map/all_to_all | solution.py:85
  386.7 4.9 %copy-start.3 = (f32[64,128]{1,0:T(8,128)S(1)}, f32[64,128]{1,0:T(8,128)}, u32[]{:S(2)}) copy-start(f32[64,128]{1,0:T(8,128)} %param.11) | copy-start | bytes 98308
Sparse Core Ops, SparseCore 0:
  115.3 169.4 all-gather.3
where the time goes:
time: 405 us; the launch traced here: 404 us
  waiting for transfers between devices  203 us (50%)
  blocking collectives  56.2 us (14%)
  other arithmetic  47.2 us (12%)
  matrix products  45.1 us (11%)
  local copies, waits for them, and re-layouts  21.3 us (5%)
  starting transfers between devices  16.4 us (4%)
  between operations  13.6 us (3%)
    all_gather x1, waiting for transfers between devices, prefix_2(): gathered = jax.tree.map(lambda a: lax.all_gather(a, axis), part)  126 us
    all_to_all x1, blocking collectives, shards(): lax.all_to_all(attended, 'head', split_axis=0, concat_axis=1, tiled=True)  37.7 us
    all_to_all x1, waiting for transfers between devices, shards(): lax.all_to_all(keys_g, 'head', split_axis=1, concat_axis=0, tiled=True)  31.3 us
    all_to_all x1, waiting for transfers between devices, shards(): lax.all_to_all(values_g, 'head', split_axis=1, concat_axis=0, tiled=True)  30.5 us
    add x15, other arithmetic, join_states(): jnp.exp(later[0])[:, None, None] * earlier[1] + later[1]  29.6 us
    all_gather x1, blocking collectives, prefix_2(): gathered = jax.tree.map(lambda a: lax.all_gather(a, axis), part)  18.6 us
    dot_general x1, matrix products, attend(): jnp.einsum('shd,she->hde', scaled_keys, value_act, preferred_element_type...  16.5 us
    dot_general x1, matrix products, attend(): jnp.einsum('hts,shd->thd', weights, value_act, preferred_element_type=jnp...  16.4 us
  transfers between devices with their start and end apart: 5, of which 4 were waited for; matrix products, arithmetic and copies ran while one was open for 4% of the time, Pallas kernels for 0%

commit v1 on v0

v1 whole, which is shorter than its diff:
```python
import functools

import jax
import jax.numpy as jnp
from jax import lax
from jax.experimental import pallas as pl
from jax.experimental.pallas import tpu as pltpu
from jax.sharding import PartitionSpec as P

F32, BF16 = jnp.float32, jnp.bfloat16
MESH = pl.DeviceIdType.MESH
TILE = 128


def plan(n_ctx, n_head, heads):
    inner = 1
    for option in (2, 4):
        if n_ctx % option == 0 and heads % (option * n_head) == 0:
            inner = option
    group = inner * n_head
    per_owner = heads // group
    chunks = 1
    for option in (2, 4):
        if per_owner % option == 0 and (heads // option) % 16 == 0:
            chunks = option
    return inner, group, per_owner, chunks


def silu(x):
    half = 0.5 * x
    return half + half * jnp.tanh(half)


def kernel(
    n_ctx, n_head, q_hbm, k_hbm, v_hbm, dec_ref, mix_ref,
    q_in, k_in, v_in, tmp_a, tmp_b, q_hm, k_hm, v_hm, cum_b, cum_t, end_b, intra,
    ends, ends_in, s_out, s_in, pre, x_in, x_out, i_out, i_in, mix,
    in_sem, e_send, e_recv, s_send, s_recv, x_send, x_recv, i_send, i_recv, o_sem,
):
    rows, heads, dim = q_hbm.shape
    inner, group, per_owner, chunks = plan(n_ctx, n_head, heads)
    width = heads // chunks
    hc = per_owner // chunks
    planes = n_ctx // inner
    ctx, head = lax.axis_index("ctx"), lax.axis_index("head")
    plane = ctx // inner
    me = (ctx % inner) * n_head + head

    def device(peer):
        return (plane * inner + peer // n_head, peer % n_head)

    def peer_at(step):
        return lax.rem(me + step, group)

    def load(source, held, at, c):
        return pltpu.make_async_copy(
            source.at[:, pl.ds(c * width, width), :], held.at[c], in_sem.at[at, c]
        )

    for c in range(chunks):
        load(k_hbm, k_in, 0, c).start()
        load(v_hbm, v_in, 1, c).start()
    for c in range(chunks):
        load(q_hbm, q_in, 2, c).start()

    barrier = pltpu.get_barrier_semaphore()

    def greet(step, carry):
        pl.semaphore_signal(barrier, inc=1, device_id=device(peer_at(step)), device_id_type=MESH)
        return carry

    lax.fori_loop(1, group, greet, 0)
    if planes > 1:
        @pl.when(plane > 0)
        def _():
            pl.semaphore_signal(barrier, inc=1, device_id=(ctx - inner, head), device_id_type=MESH)

        @pl.when(plane < planes - 1)
        def _():
            pl.semaphore_signal(barrier, inc=1, device_id=(ctx + inner, head), device_id_type=MESH)

    decays = dec_ref[...]
    t_at = lax.broadcasted_iota(jnp.int32, (rows, rows), 0)
    s_at = lax.broadcasted_iota(jnp.int32, (rows, rows), 1)
    lower = jnp.where(s_at <= t_at, 1.0, 0.0).astype(BF16)
    upper = jnp.where(t_at <= s_at, 1.0, 0.0).astype(BF16)
    over_rows = (((0,), (0,)), ((), ()))
    cum_t[...] = lax.dot_general(decays, upper, over_rows, preferred_element_type=F32)
    end_b[...] = lax.dot_general(
        decays, jnp.ones((rows, dim), BF16), over_rows, preferred_element_type=F32
    )
    for o in range(group):
        for c in range(chunks):
            at = c * width + o * hc
            ends[o, c * hc : (c + 1) * hc, :] = end_b[at : at + hc, :]
    some = 8
    h_at = lax.broadcasted_iota(jnp.int32, (heads, some * dim), 0)
    l_at = lax.broadcasted_iota(jnp.int32, (heads, some * dim), 1) // dim

    def spread(g, carry):
        pick = jnp.where(h_at == l_at + g * some, 1.0, 0.0).astype(BF16)
        wide = jnp.dot(decays, pick, preferred_element_type=F32).astype(BF16)
        summed = jnp.dot(lower, wide, preferred_element_type=F32)
        for i in range(some):
            cum_b[g * some + i] = summed[:, i * dim : (i + 1) * dim]
        return carry

    lax.fori_loop(0, heads // some, spread, 0)

    greetings = group - 1
    if planes > 1:
        greetings = greetings + jnp.where(plane > 0, 1, 0) + jnp.where(plane < planes - 1, 1, 0)
    pl.semaphore_wait(barrier, greetings)

    def remote(src, dst, send, recv, to):
        return pltpu.make_async_remote_copy(
            src_ref=src, dst_ref=dst, send_sem=send, recv_sem=recv,
            device_id=to, device_id_type=MESH,
        )

    def end_copy(peer, slot):
        return remote(ends.at[peer], ends_in.at[slot], e_send.at[peer], e_recv.at[slot], device(peer))

    def s_copy(c, peer, slot):
        return remote(
            s_out.at[c, peer], s_in.at[c, slot], s_send.at[c, peer], s_recv.at[c, slot], device(peer)
        )

    def i_copy(c, peer, slot):
        return remote(
            i_out.at[c, peer], i_in.at[c, slot], i_send.at[c, peer], i_recv.at[c, slot], device(peer)
        )

    def x_copy(c):
        return remote(
            x_out.at[c], x_in.at[c], x_send.at[c], x_recv.at[c],
            (lax.rem(ctx + inner, n_ctx), head),
        )

    def each_peer(body):
        def one(step, carry):
            body(peer_at(step))
            return carry

        lax.fori_loop(1, group, one, 0)

    each_peer(lambda peer: end_copy(peer, me).start())
    ends_in[me] = ends[me]

    step_rows = 16

    def activate(held, c, tmp):
        def some_rows(b, carry):
            x = held[c, pl.ds(b * step_rows, step_rows)].astype(F32)
            tmp[pl.ds(b * step_rows * width, step_rows * width), :] = silu(x).reshape(
                step_rows * width, dim
            )
            return carry

        lax.fori_loop(0, rows // step_rows, some_rows, 0)

    unroll = 4

    def each_head(c, body):
        def one(g, carry):
            for u in range(unroll):
                i = g * unroll + u
                body(i, c * width + i)
            return carry

        lax.fori_loop(0, width // unroll, one, 0)

    def states(c):
        load(k_hbm, k_in, 0, c).wait()
        load(v_hbm, v_in, 1, c).wait()
        activate(k_in, c, tmp_a)
        activate(v_in, c, tmp_b)

        def one(i, h):
            key = tmp_a[pl.ds(i, rows, stride=width), :].astype(BF16)
            value = tmp_b[pl.ds(i, rows, stride=width), :].astype(BF16)
            k_hm[h] = key
            v_hm[h] = value
            fade = jnp.exp(end_b[pl.ds(h, 1), :] - cum_b[h])
            scaled = (key.astype(F32) * fade).astype(BF16)
            state = lax.dot_general(scaled, value, over_rows, preferred_element_type=F32)
            s_out[c, i // hc, pl.ds((i % hc) * dim, dim), :] = state.astype(BF16)

        each_head(c, one)
        each_peer(lambda peer: s_copy(c, peer, me).start())
        s_in[c, me] = s_out[c, me]

    def inside(c):
        load(q_hbm, q_in, 2, c).wait()
        activate(q_in, c, tmp_a)

        def one(i, h):
            query = tmp_a[pl.ds(i, rows, stride=width), :].astype(BF16)
            q_hm[h] = query
            key, value, cum = k_hm[h], v_hm[h], cum_b[h]
            row = cum_t[pl.ds(h, 1), :]
            outs = []
            for s0 in range(0, rows, TILE):
                w = min(TILE, rows - s0)
                n = rows - s0
                scores = lax.dot_general(
                    query[s0:], key[s0 : s0 + w], (((1,), (1,)), ((), ())),
                    preferred_element_type=F32,
                )
                offset = cum[s0:, :w] - row[:, s0 : s0 + w]
                tt = lax.broadcasted_iota(jnp.int32, (n, w), 0)
                ss = lax.broadcasted_iota(jnp.int32, (n, w), 1)
                weights = scores * jnp.exp(jnp.where(ss <= tt, offset, -1e30))
                outs.append(
                    jnp.dot(
                        weights.astype(BF16), value[s0 : s0 + w], preferred_element_type=F32
                    )
                )
            intra[h] = outs[0]
            for at in range(1, len(outs)):
                intra[h, at * TILE :, :] += outs[at]

        each_head(c, one)

    def join(c):
        each_peer(lambda peer: s_copy(c, peer, peer).wait_recv())

        def decay_of(j, i):
            return jnp.exp(ends_in[j, c * hc + i : c * hc + i + 1, :])

        for i in range(hc):
            part = pl.ds(i * dim, dim)
            total = s_in[c, 0, part, :].astype(F32)
            for j in range(1, group):
                pre[j, part, :] = total
                total = decay_of(j, i) * total + s_in[c, j, part, :].astype(F32)
            x_out[c, part, :] = total

        if planes > 1:
            @pl.when(plane > 0)
            def _():
                x_copy(c).wait_recv()
                for i in range(hc):
                    part = pl.ds(i * dim, dim)
                    fade = jnp.sum(ends_in[:, c * hc + i, :], axis=0, keepdims=True)
                    x_out[c, part, :] += jnp.exp(fade) * x_in[c, part, :]

            @pl.when(plane == 0)
            def _():
                x_in[c] = jnp.zeros(x_in.shape[1:], F32)

            @pl.when(plane < planes - 1)
            def _():
                x_copy(c).start()
        else:
            x_in[c] = jnp.zeros(x_in.shape[1:], F32)

        for i in range(hc):
            part = pl.ds(i * dim, dim)
            come = x_in[c, part, :]
            i_out[c, 0, part, :] = come.astype(BF16)
            fade = jnp.zeros((1, dim), F32)
            for j in range(1, group):
                fade = fade + ends_in[j - 1, c * hc + i : c * hc + i + 1, :]
                i_out[c, j, part, :] = (pre[j, part, :] + jnp.exp(fade) * come).astype(BF16)
        each_peer(lambda peer: i_copy(c, peer, me).start())
        i_in[c, me] = i_out[c, me]

    def finish(c):
        each_peer(lambda peer: i_copy(c, peer, peer).wait_recv())

        def one(i, h):
            come = i_in[c, i // hc, pl.ds((i % hc) * dim, dim), :]
            inter = jnp.dot(q_hm[h], come, preferred_element_type=F32)
            mix[pl.ds(h, rows, stride=heads), :] = intra[h] + inter * jnp.exp(cum_b[h])

        each_head(c, one)

    for c in range(chunks):
        states(c)
    each_peer(lambda peer: end_copy(peer, peer).wait_recv())
    for c in range(chunks):
        inside(c)
        join(c)
    for c in range(chunks):
        finish(c)

    def give(b, carry):
        span = step_rows * heads
        mix_ref[pl.ds(b * step_rows, step_rows)] = (
            mix[pl.ds(b * span, span), :].reshape(step_rows, heads, dim).astype(BF16)
        )
        return carry

    lax.fori_loop(0, rows // step_rows, give, 0)

    each_peer(lambda peer: end_copy(peer, me).wait_send())
    for c in range(chunks):
        each_peer(lambda peer: s_copy(c, peer, me).wait_send())
        each_peer(lambda peer: i_copy(c, peer, me).wait_send())
    if planes > 1:
        @pl.when(plane < planes - 1)
        def _():
            for c in range(chunks):
                x_copy(c).wait_send()


def normalize(mixed, out_gain):
    values32 = mixed.astype(F32)
    meansq = jnp.mean(values32 * values32, axis=(1, 2), keepdims=True)
    return (values32 * lax.rsqrt(meansq + 1e-06) * out_gain[None]).astype(BF16)


def shards(n_ctx, n_head, queries, keys, values, decay_log, out_gain):
    rows, heads, dim = queries.shape
    inner, group, per_owner, chunks = plan(n_ctx, n_head, heads)
    width, hc = heads // chunks, per_owner // chunks
    held = pltpu.VMEM((chunks, rows, width, dim), BF16)
    major = pltpu.VMEM((heads, rows, dim), BF16)
    block = (hc * dim, dim)
    dma = pltpu.SemaphoreType.DMA
    mixed = pl.pallas_call(
        functools.partial(kernel, n_ctx, n_head),
        out_shape=jax.ShapeDtypeStruct((rows, heads, dim), BF16),
        in_specs=[pl.BlockSpec(memory_space=pl.ANY)] * 3 + [pl.BlockSpec(memory_space=pltpu.VMEM)],
        out_specs=pl.BlockSpec(memory_space=pltpu.VMEM),
        scratch_shapes=[
            held, held, held,
            pltpu.VMEM((rows * width, dim), F32), pltpu.VMEM((rows * width, dim), F32),
            major, major, major,
            pltpu.VMEM((heads, rows, dim), F32),
            pltpu.VMEM((heads, rows), F32),
            pltpu.VMEM((heads, dim), F32),
            pltpu.VMEM((heads, rows, dim), F32),
            pltpu.VMEM((group, max(8, per_owner), dim), F32),
            pltpu.VMEM((group, max(8, per_owner), dim), F32),
            pltpu.VMEM((chunks, group) + block, BF16), pltpu.VMEM((chunks, group) + block, BF16),
            pltpu.VMEM((group,) + block, F32),
            pltpu.VMEM((chunks,) + block, F32), pltpu.VMEM((chunks,) + block, F32),
            pltpu.VMEM((chunks, group) + block, BF16), pltpu.VMEM((chunks, group) + block, BF16),
            pltpu.VMEM((rows * heads, dim), F32),
            dma((3, chunks)),
            dma((group,)), dma((group,)),
            dma((chunks, group)), dma((chunks, group)),
            dma((chunks,)), dma((chunks,)),
            dma((chunks, group)), dma((chunks, group)),
            dma,
        ],
        compiler_params=pltpu.CompilerParams(
            collective_id=0, has_side_effects=True, vmem_limit_bytes=60 * 2**20
        ),
        cost_estimate=pl.CostEstimate(
            flops=8 * rows * heads * dim * dim,
            bytes_accessed=8 * rows * heads * dim,
            transcendentals=0,
        ),
    )(queries, keys, values, decay_log)
    return normalize(mixed, out_gain)


def solution(mesh):
    return jax.shard_map(
        functools.partial(shards, mesh.shape["ctx"], mesh.shape["head"]),
        mesh=mesh,
        in_specs=(
            P(("ctx", "head"), None, None),
            P(("ctx", "head"), None, None),
            P(("ctx", "head"), None, None),
            P(("ctx", "head"), None),
            P(),
        ),
        out_specs=P(("ctx", "head"), None, None),
        check_vma=False,
    )
```

time: 405 us -> 69.2 us (0.17)
  the two profiles are of different devices: /device:TPU:27 before, /device:TPU:1 now
where the time goes in v1:
time: 69.2 us; the launch traced here: 68.8 us
  Pallas kernels  61.5 us (89%)
  other arithmetic  5.78 us (8%)
  local copies, waits for them, and re-layouts  1.49 us (2%)
    pallas_call x1, Pallas kernels, shards(): pl.pallas_call(functools.partial(kernel, n_ctx, n_head), out_shape=jax.Sh...  61.5 us
    reduce_sum x1, other arithmetic, normalize(): meansq = jnp.mean(values32 * values32, axis=(1, 2), keepdims=True)  3.22 us
    convert_element_type x1, other arithmetic, normalize(): return (values32 * lax.rsqrt(meansq + 1e-06) * out_gain[None]).astype(BF16)  2.55 us
    unnamed x5, local copies, waits for them, and re-layouts  1.49 us

profile of v1, /device:TPU:1, one launch (start us, length us, event | category | flops | bytes accessed | tf_op | source)
XLA Modules:
  0.0 68.8 jit_solution(9901812245307877043)
XLA Ops:
  0.0 1.5 %copy.6.dec_ref = bf16[192,64]{1,0:T(8,128)(2,1)} copy(bf16[192,64]{0,1:T(8,128)(2,1)} %param.8) | data formatting | bytes 49152 | tf_op args[3]
  1.5 0.0 copy-start.1
  1.5 61.5 %shard_map.55 = bf16[192,64,128]{2,1,0:T(8,128)(2,1)} custom-call(bf16[192,64,128]{2,1,0:T(8,128)(2,1)} %q_hbm.1, bf16[192,64,128]{2,1,0:T(8,128)(2,1)} %k_hbm.1, bf16[192,64,128]{2,1,0:T(8,128)(2,1)} %v_hbm.1, bf16[192,64]{1,0:T(8,128)(2,1)} %copy.6.dec_ref), custom_call_target="tpu_custom_call" | custom-call | flops 1610612736 | bytes 12582912 | tf_op jit(solution)/shard_map/pallas_call | solution.py:322
  63.0 0.0 copy-start
  63.0 3.2 %fusion = f32[192]{0:T(256)S(1)} fusion(bf16[192,64,128]{2,1,0:T(8,128)(2,1)} %shard_map.55), kind=kLoop, calls=%fused_computation.2 | loop fusion | flops 4718400 | bytes 3146496 | tf_op jit(solution)/shard_map/reduce_sum | solution.py:310
  66.2 0.0 copy-done.1
  66.2 0.0 copy-done
  66.2 2.5 %fusion.2 = bf16[192,64,128]{2,1,0:T(8,128)(2,1)} fusion(bf16[192,64,128]{2,1,0:T(8,128)(2,1)S(1)} %copy-done, f32[64,128]{1,0:T(8,128)S(1)} %copy-done.1, f32[192]{0:T(256)S(1)} %add_rsqrt_fusion), kind=kLoop, calls=%fused_computation.4 | loop fusion | flops 6291456 | bytes 6324992 | tf_op jit(solution)/shard_map/convert_element_type | solution.py:311
  (1 shorter events, 0.0 us)
Async XLA Ops:
  1.5 64.7 %copy-start.1 = (f32[64,128]{1,0:T(8,128)S(1)}, f32[64,128]{1,0:T(8,128)}, u32[]{:S(2)}) copy-start(f32[64,128]{1,0:T(8,128)} %param.9) | copy-start | bytes 98308
  63.0 3.2 %copy-start = (bf16[192,64,128]{2,1,0:T(8,128)(2,1)S(1)}, bf16[192,64,128]{2,1,0:T(8,128)(2,1)}, u32[]{:S(2)}) copy-start(bf16[192,64,128]{2,1,0:T(8,128)(2,1)} %shard_map.55) | copy-start | bytes 9437188

commit v2 on v1

--- a/solution.py
+++ b/solution.py
@@ -32,10 +32,10 @@
 
 
 def kernel(
-    n_ctx, n_head, q_hbm, k_hbm, v_hbm, dec_ref, mix_ref,
+    n_ctx, n_head, q_hbm, k_hbm, v_hbm, dec_ref, mix_hbm, scale_ref,
     q_in, k_in, v_in, tmp_a, tmp_b, q_hm, k_hm, v_hm, cum_b, cum_t, end_b, intra,
-    ends, ends_in, s_out, s_in, pre, x_in, x_out, i_out, i_in, mix,
-    in_sem, e_send, e_recv, s_send, s_recv, x_send, x_recv, i_send, i_recv, o_sem,
+    ends, ends_in, s_out, s_in, pre, tot_out, tot_in, t_out, t_in, come_x, i_out, i_in, squares,
+    in_sem, e_send, e_recv, s_send, s_recv, d_send, d_recv, t_send, t_recv, i_send, i_recv, o_sem,
 ):
     rows, heads, dim = q_hbm.shape
     inner, group, per_owner, chunks = plan(n_ctx, n_head, heads)
@@ -44,7 +44,8 @@
     planes = n_ctx // inner
     ctx, head = lax.axis_index("ctx"), lax.axis_index("head")
     plane = ctx // inner
-    me = (ctx % inner) * n_head + head
+    place = ctx % inner
+    me = place * n_head + head
 
     def device(peer):
         return (plane * inner + peer // n_head, peer % n_head)
@@ -70,14 +71,15 @@
         return carry
 
     lax.fori_loop(1, group, greet, 0)
-    if planes > 1:
-        @pl.when(plane > 0)
-        def _():
-            pl.semaphore_signal(barrier, inc=1, device_id=(ctx - inner, head), device_id_type=MESH)
-
-        @pl.when(plane < planes - 1)
-        def _():
-            pl.semaphore_signal(barrier, inc=1, device_id=(ctx + inner, head), device_id_type=MESH)
+
+    def greet_plane(step, carry):
+        other = lax.rem(plane + step, planes)
+        pl.semaphore_signal(
+            barrier, inc=1, device_id=(other * inner + place, head), device_id_type=MESH
+        )
+        return carry
+
+    lax.fori_loop(1, planes, greet_plane, 0)
 
     decays = dec_ref[...]
     t_at = lax.broadcasted_iota(jnp.int32, (rows, rows), 0)
@@ -85,33 +87,27 @@
     lower = jnp.where(s_at <= t_at, 1.0, 0.0).astype(BF16)
     upper = jnp.where(t_at <= s_at, 1.0, 0.0).astype(BF16)
     over_rows = (((0,), (0,)), ((), ()))
-    cum_t[...] = lax.dot_general(decays, upper, over_rows, preferred_element_type=F32)
-    end_b[...] = lax.dot_general(
-        decays, jnp.ones((rows, dim), BF16), over_rows, preferred_element_type=F32
-    )
+    cum_t[...] = jnp.dot(decays, upper, preferred_element_type=F32)
+    end_b[...] = jnp.dot(decays, jnp.ones((rows, dim), BF16), preferred_element_type=F32)
     for o in range(group):
         for c in range(chunks):
             at = c * width + o * hc
             ends[o, c * hc : (c + 1) * hc, :] = end_b[at : at + hc, :]
+    squares[...] = jnp.zeros_like(squares)
     some = 8
     h_at = lax.broadcasted_iota(jnp.int32, (heads, some * dim), 0)
     l_at = lax.broadcasted_iota(jnp.int32, (heads, some * dim), 1) // dim
 
     def spread(g, carry):
         pick = jnp.where(h_at == l_at + g * some, 1.0, 0.0).astype(BF16)
-        wide = jnp.dot(decays, pick, preferred_element_type=F32).astype(BF16)
+        wide = lax.dot_general(
+            decays, pick, over_rows, preferred_element_type=F32
+        ).astype(BF16)
         summed = jnp.dot(lower, wide, preferred_element_type=F32)
         for i in range(some):
             cum_b[g * some + i] = summed[:, i * dim : (i + 1) * dim]
         return carry
 
-    lax.fori_loop(0, heads // some, spread, 0)
-
-    greetings = group - 1
-    if planes > 1:
-        greetings = greetings + jnp.where(plane > 0, 1, 0) + jnp.where(plane < planes - 1, 1, 0)
-    pl.semaphore_wait(barrier, greetings)
-
     def remote(src, dst, send, recv, to):
         return pltpu.make_async_remote_copy(
             src_ref=src, dst_ref=dst, send_sem=send, recv_sem=recv,
@@ -131,10 +127,17 @@
             i_out.at[c, peer], i_in.at[c, slot], i_send.at[c, peer], i_recv.at[c, slot], device(peer)
         )
 
-    def x_copy(c):
+    def at_plane(other):
+        return (other * inner + place, head)
+
+    def d_copy(step, slot):
+        other = lax.rem(plane + step, planes)
+        return remote(tot_out, tot_in.at[slot], d_send.at[step], d_recv.at[slot], at_plane(other))
+
+    def t_copy(c, step, slot):
+        other = lax.rem(plane + step, planes)
         return remote(
-            x_out.at[c], x_in.at[c], x_send.at[c], x_recv.at[c],
-            (lax.rem(ctx + inner, n_ctx), head),
+            t_out.at[c], t_in.at[c, slot], t_send.at[c, step], t_recv.at[c, slot], at_plane(other)
         )
 
     def each_peer(body):
@@ -144,8 +147,17 @@
 
         lax.fori_loop(1, group, one, 0)
 
-    each_peer(lambda peer: end_copy(peer, me).start())
-    ends_in[me] = ends[me]
+    def later_planes(body):
+        for step in range(1, planes):
+            @pl.when(plane + step < planes)
+            def _():
+                body(step)
+
+    def earlier_planes(body):
+        for p in range(planes - 1):
+            @pl.when(p < plane)
+            def _():
+                body(p)
 
     step_rows = 16
 
@@ -171,6 +183,7 @@
         lax.fori_loop(0, width // unroll, one, 0)
 
     def states(c):
+        lax.fori_loop(c * width // some, (c + 1) * width // some, spread, 0)
         load(k_hbm, k_in, 0, c).wait()
         load(v_hbm, v_in, 1, c).wait()
         activate(k_in, c, tmp_a)
@@ -187,6 +200,10 @@
             s_out[c, i // hc, pl.ds((i % hc) * dim, dim), :] = state.astype(BF16)
 
         each_head(c, one)
+        if c == 0:
+            pl.semaphore_wait(barrier, group + planes - 2)
+            each_peer(lambda peer: end_copy(peer, me).start())
+            ends_in[me] = ends[me]
         each_peer(lambda peer: s_copy(c, peer, me).start())
         s_in[c, me] = s_out[c, me]
 
@@ -223,48 +240,52 @@
         each_head(c, one)
 
     def join(c):
+        if c == 0:
+            each_peer(lambda peer: end_copy(peer, peer).wait_recv())
+            tot_out[...] = jnp.sum(ends_in[...], axis=0)
+            later_planes(lambda step: d_copy(step, plane).start())
         each_peer(lambda peer: s_copy(c, peer, peer).wait_recv())
-
-        def decay_of(j, i):
-            return jnp.exp(ends_in[j, c * hc + i : c * hc + i + 1, :])
-
         for i in range(hc):
             part = pl.ds(i * dim, dim)
+            at = c * hc + i
             total = s_in[c, 0, part, :].astype(F32)
             for j in range(1, group):
-                pre[j, part, :] = total
-                total = decay_of(j, i) * total + s_in[c, j, part, :].astype(F32)
-            x_out[c, part, :] = total
-
-        if planes > 1:
-            @pl.when(plane > 0)
-            def _():
-                x_copy(c).wait_recv()
-                for i in range(hc):
-                    part = pl.ds(i * dim, dim)
-                    fade = jnp.sum(ends_in[:, c * hc + i, :], axis=0, keepdims=True)
-                    x_out[c, part, :] += jnp.exp(fade) * x_in[c, part, :]
-
-            @pl.when(plane == 0)
-            def _():
-                x_in[c] = jnp.zeros(x_in.shape[1:], F32)
-
-            @pl.when(plane < planes - 1)
-            def _():
-                x_copy(c).start()
-        else:
-            x_in[c] = jnp.zeros(x_in.shape[1:], F32)
-
+                pre[c, j, part, :] = total
+                fade = jnp.exp(ends_in[j, at : at + 1, :])
+                total = fade * total + s_in[c, j, part, :].astype(F32)
+            t_out[c, part, :] = total.astype(BF16)
+        later_planes(lambda step: t_copy(c, step, plane).start())
+
+    def spread_out(c):
+        if c == 0:
+            earlier_planes(lambda p: d_copy(1, p).wait_recv())
+        earlier_planes(lambda p: t_copy(c, 1, p).wait_recv())
+        come_x[...] = jnp.zeros_like(come_x)
+
+        def add(p):
+            for i in range(hc):
+                part = pl.ds(i * dim, dim)
+                at = c * hc + i
+                fade = jnp.exp(tot_in[p, at : at + 1, :])
+                come_x[part, :] = fade * come_x[part, :] + t_in[c, p, part, :].astype(F32)
+
+        earlier_planes(add)
         for i in range(hc):
             part = pl.ds(i * dim, dim)
-            come = x_in[c, part, :]
+            at = c * hc + i
+            come = come_x[part, :]
             i_out[c, 0, part, :] = come.astype(BF16)
             fade = jnp.zeros((1, dim), F32)
             for j in range(1, group):
-                fade = fade + ends_in[j - 1, c * hc + i : c * hc + i + 1, :]
-                i_out[c, j, part, :] = (pre[j, part, :] + jnp.exp(fade) * come).astype(BF16)
+                fade = fade + ends_in[j - 1, at : at + 1, :]
+                i_out[c, j, part, :] = (pre[c, j, part, :] + jnp.exp(fade) * come).astype(BF16)
         each_peer(lambda peer: i_copy(c, peer, me).start())
         i_in[c, me] = i_out[c, me]
+
+    def give(c):
+        return pltpu.make_async_copy(
+            q_in.at[c], mix_hbm.at[:, pl.ds(c * width, width), :], o_sem.at[c]
+        )
 
     def finish(c):
         each_peer(lambda peer: i_copy(c, peer, peer).wait_recv())
@@ -272,43 +293,46 @@
         def one(i, h):
             come = i_in[c, i // hc, pl.ds((i % hc) * dim, dim), :]
             inter = jnp.dot(q_hm[h], come, preferred_element_type=F32)
-            mix[pl.ds(h, rows, stride=heads), :] = intra[h] + inter * jnp.exp(cum_b[h])
+            mixed = (intra[h] + inter * jnp.exp(cum_b[h])).astype(BF16).astype(F32)
+            squares[...] += mixed * mixed
+            tmp_a[pl.ds(i, rows, stride=width), :] = mixed
 
         each_head(c, one)
 
+        def some_rows(b, carry):
+            span = step_rows * width
+            q_in[c, pl.ds(b * step_rows, step_rows)] = (
+                tmp_a[pl.ds(b * span, span), :].reshape(step_rows, width, dim).astype(BF16)
+            )
+            return carry
+
+        lax.fori_loop(0, rows // step_rows, some_rows, 0)
+        give(c).start()
+
     for c in range(chunks):
         states(c)
-    each_peer(lambda peer: end_copy(peer, peer).wait_recv())
-    for c in range(chunks):
+    for c in range(chunks):
+        join(c)
         inside(c)
-        join(c)
+        if c > 0:
+            spread_out(c - 1)
+    spread_out(chunks - 1)
     for c in range(chunks):
         finish(c)
-
-    def give(b, carry):
-        span = step_rows * heads
-        mix_ref[pl.ds(b * step_rows, step_rows)] = (
-            mix[pl.ds(b * span, span), :].reshape(step_rows, heads, dim).astype(BF16)
-        )
-        return carry
-
-    lax.fori_loop(0, rows // step_rows, give, 0)
+    meansq = jnp.sum(squares[...], axis=1, keepdims=True) * (1.0 / (heads * dim))
+    scale_ref[...] = jnp.broadcast_to(lax.rsqrt(meansq + 1e-06), scale_ref.shape)
 
     each_peer(lambda peer: end_copy(peer, me).wait_send())
+    later_planes(lambda step: d_copy(step, plane).wait_send())
     for c in range(chunks):
         each_peer(lambda peer: s_copy(c, peer, me).wait_send())
         each_peer(lambda peer: i_copy(c, peer, me).wait_send())
-    if planes > 1:
-        @pl.when(plane < planes - 1)
-        def _():
-            for c in range(chunks):
-                x_copy(c).wait_send()
-
-
-def normalize(mixed, out_gain):
-    values32 = mixed.astype(F32)
-    meansq = jnp.mean(values32 * values32, axis=(1, 2), keepdims=True)
-    return (values32 * lax.rsqrt(meansq + 1e-06) * out_gain[None]).astype(BF16)
+        later_planes(lambda step: t_copy(c, step, plane).wait_send())
+        give(c).wait()
+
+
+def normalize(mixed, scale, out_gain):
+    return (mixed.astype(F32) * scale[:, None, :] * out_gain[None]).astype(BF16)
 
 
 def shards(n_ctx, n_head, queries, keys, values, decay_log, out_gain):
@@ -319,11 +343,16 @@
     major = pltpu.VMEM((heads, rows, dim), BF16)
     block = (hc * dim, dim)
     dma = pltpu.SemaphoreType.DMA
-    mixed = pl.pallas_call(
+    planes = n_ctx // inner
+    tile = (max(8, per_owner), dim)
+    mixed, scale = pl.pallas_call(
         functools.partial(kernel, n_ctx, n_head),
-        out_shape=jax.ShapeDtypeStruct((rows, heads, dim), BF16),
+        out_shape=(
+            jax.ShapeDtypeStruct((rows, heads, dim), BF16),
+            jax.ShapeDtypeStruct((rows, dim), F32),
+        ),
         in_specs=[pl.BlockSpec(memory_space=pl.ANY)] * 3 + [pl.BlockSpec(memory_space=pltpu.VMEM)],
-        out_specs=pl.BlockSpec(memory_space=pltpu.VMEM),
+        out_specs=(pl.BlockSpec(memory_space=pl.ANY), pl.BlockSpec(memory_space=pltpu.VMEM)),
         scratch_shapes=[
             held, held, held,
             pltpu.VMEM((rows * width, dim), F32), pltpu.VMEM((rows * width, dim), F32),
@@ -332,19 +361,21 @@
             pltpu.VMEM((heads, rows), F32),
             pltpu.VMEM((heads, dim), F32),
             pltpu.VMEM((heads, rows, dim), F32),
-            pltpu.VMEM((group, max(8, per_owner), dim), F32),
-            pltpu.VMEM((group, max(8, per_owner), dim), F32),
+            pltpu.VMEM((group,) + tile, F32), pltpu.VMEM((group,) + tile, F32),
             pltpu.VMEM((chunks, group) + block, BF16), pltpu.VMEM((chunks, group) + block, BF16),
-            pltpu.VMEM((group,) + block, F32),
-            pltpu.VMEM((chunks,) + block, F32), pltpu.VMEM((chunks,) + block, F32),
+            pltpu.VMEM((chunks, group) + block, F32),
+            pltpu.VMEM(tile, F32), pltpu.VMEM((planes,) + tile, F32),
+            pltpu.VMEM((chunks,) + block, BF16), pltpu.VMEM((chunks, planes) + block, BF16),
+            pltpu.VMEM(block, F32),
             pltpu.VMEM((chunks, group) + block, BF16), pltpu.VMEM((chunks, group) + block, BF16),
-            pltpu.VMEM((rows * heads, dim), F32),
+            pltpu.VMEM((rows, dim), F32),
             dma((3, chunks)),
             dma((group,)), dma((group,)),
             dma((chunks, group)), dma((chunks, group)),
-            dma((chunks,)), dma((chunks,)),
+            dma((planes,)), dma((planes,)),
+            dma((chunks, planes)), dma((chunks, planes)),
             dma((chunks, group)), dma((chunks, group)),
-            dma,
+            dma((chunks,)),
         ],
         compiler_params=pltpu.CompilerParams(
             collective_id=0, has_side_effects=True, vmem_limit_bytes=60 * 2**20
@@ -354,8 +385,8 @@
             bytes_accessed=8 * rows * heads * dim,
             transcendentals=0,
         ),
-    )(queries, keys, values, decay_log)
-    return normalize(mixed, out_gain)
+    )(queries, keys, values, decay_log.T)
+    return normalize(mixed, scale, out_gain)
 
 
 def solution(mesh):

time: 69.2 us -> 63.2 us (0.913)
  Pallas kernels: 61.5 us -> 58.1 us
  local copies, waits for them, and re-layouts: 1.49 us -> 0.01 us
  other arithmetic: 5.78 us -> 4.58 us
    pallas_call x1, Pallas kernels: 61.5 us -> 58.1 us  [shards(): pl.pallas_call(functools.partial(kernel, n_ctx, n_head), out_shape=(jax.S...]
    reduce_sum x1 -> x0, other arithmetic: 3.22 us -> none  [normalize(): meansq = jnp.mean(values32 * values32, axis=(1, 2), keepdims=True)]
    convert_element_type x1, other arithmetic: 2.55 us -> 4.58 us  [normalize(): return (mixed.astype(F32) * scale[:, None, :] * out_gain[None]).astype(BF16)]
    unnamed x5 -> x2, local copies, waits for them, and re-layouts: 1.49 us -> 0.01 us
where the time goes in v2:
time: 63.2 us; the launch traced here: 62.7 us
  Pallas kernels  58.1 us (92%)
  other arithmetic  4.58 us (7%)
    pallas_call x1, Pallas kernels, shards(): pl.pallas_call(functools.partial(kernel, n_ctx, n_head), out_shape=(jax.S...  58.1 us
    convert_element_type x1, other arithmetic, normalize(): return (mixed.astype(F32) * scale[:, None, :] * out_gain[None]).astype(BF16)  4.58 us

profile of v2, /device:TPU:1, one launch (start us, length us, event | category | flops | bytes accessed | tf_op | source)
XLA Modules:
  0.0 62.7 jit_solution(1494002680331403448)
XLA Ops:
  0.0 0.0 copy-start
  0.0 58.1 %shard_map.55 = (bf16[192,64,128]{2,1,0:T(8,128)(2,1)}, f32[192,128]{1,0:T(8,128)}) custom-call(bf16[192,64,128]{2,1,0:T(8,128)(2,1)} %q_hbm.1, bf16[192,64,128]{2,1,0:T(8,128)(2,1)} %k_hbm.1, bf16[192,64,128]{2,1,0:T(8,128)(2,1)} %v_hbm.1, bf16[64,192]{1,0:T(8,128)(2,1)} %bitcast.1), custom_call_target="tpu_custom_call" | custom-call | flops 1610612736 | bytes 12582912 | tf_op jit(solution)/shard_map/pallas_call | solution.py:348
  58.1 0.0 copy-done
  58.2 4.6 %multiply_convert_fusion = bf16[192,64,128]{2,1,0:T(8,128)(2,1)} fusion(bf16[192,64,128]{2,1,0:T(8,128)(2,1)} %get-tuple-element.7, f32[64,128]{1,0:T(8,128)S(1)} %copy-done, f32[192,128]{1,0:T(8,128)} %get-tuple-element.8), kind=kLoop, calls=%fused_computation | loop fusion | flops 6291456 | bytes 6422528 | tf_op jit(solution)/shard_map/convert_element_type | solution.py:335
Async XLA Ops:
  0.0 58.2 %copy-start = (f32[64,128]{1,0:T(8,128)S(1)}, f32[64,128]{1,0:T(8,128)}, u32[]{:S(2)}) copy-start(f32[64,128]{1,0:T(8,128)} %param.9) | copy-start | bytes 98308

commit v3 on v2

--- a/solution.py
+++ b/solution.py
@@ -32,9 +32,9 @@
 
 
 def kernel(
-    n_ctx, n_head, q_hbm, k_hbm, v_hbm, dec_ref, mix_hbm, scale_ref,
+    n_ctx, n_head, q_hbm, k_hbm, v_hbm, dec_ref, mix_hbm,
     q_in, k_in, v_in, tmp_a, tmp_b, q_hm, k_hm, v_hm, cum_b, cum_t, end_b, intra,
-    ends, ends_in, s_out, s_in, pre, tot_out, tot_in, t_out, t_in, come_x, i_out, i_in, squares,
+    ends, ends_in, s_out, s_in, pre, tot_out, tot_in, t_out, t_in, come_x, i_out, i_in,
     in_sem, e_send, e_recv, s_send, s_recv, d_send, d_recv, t_send, t_recv, i_send, i_recv, o_sem,
 ):
     rows, heads, dim = q_hbm.shape
@@ -58,11 +58,8 @@
             source.at[:, pl.ds(c * width, width), :], held.at[c], in_sem.at[at, c]
         )
 
-    for c in range(chunks):
-        load(k_hbm, k_in, 0, c).start()
-        load(v_hbm, v_in, 1, c).start()
-    for c in range(chunks):
-        load(q_hbm, q_in, 2, c).start()
+    load(k_hbm, k_in, 0, 0).start()
+    load(v_hbm, v_in, 1, 0).start()
 
     barrier = pltpu.get_barrier_semaphore()
 
@@ -93,7 +90,6 @@
         for c in range(chunks):
             at = c * width + o * hc
             ends[o, c * hc : (c + 1) * hc, :] = end_b[at : at + hc, :]
-    squares[...] = jnp.zeros_like(squares)
     some = 8
     h_at = lax.broadcasted_iota(jnp.int32, (heads, some * dim), 0)
     l_at = lax.broadcasted_iota(jnp.int32, (heads, some * dim), 1) // dim
@@ -182,14 +178,40 @@
 
         lax.fori_loop(0, width // unroll, one, 0)
 
+    owners = max(1, unroll // hc)
+
+    def each_owner(c, first, before, body, after):
+        def one(g, carry):
+            steps = [first + g * owners + u for u in range(owners)]
+            for step in steps:
+                before(step, peer_at(step))
+            for step in steps:
+                for u in range(hc):
+                    i = peer_at(step) * hc + u
+                    body(i, c * width + i, peer_at(step), u)
+            for step in steps:
+                after(step, peer_at(step))
+            return carry
+
+        lax.fori_loop(0, group // owners, one, 0)
+
+    def nothing(step, peer):
+        pass
+
     def states(c):
         lax.fori_loop(c * width // some, (c + 1) * width // some, spread, 0)
         load(k_hbm, k_in, 0, c).wait()
         load(v_hbm, v_in, 1, c).wait()
+        if c + 1 < chunks:
+            load(k_hbm, k_in, 0, c + 1).start()
+            load(v_hbm, v_in, 1, c + 1).start()
+        else:
+            for at in range(chunks):
+                load(q_hbm, q_in, 2, at).start()
         activate(k_in, c, tmp_a)
         activate(v_in, c, tmp_b)
 
-        def one(i, h):
+        def one(i, h, peer, u):
             key = tmp_a[pl.ds(i, rows, stride=width), :].astype(BF16)
             value = tmp_b[pl.ds(i, rows, stride=width), :].astype(BF16)
             k_hm[h] = key
@@ -197,14 +219,20 @@
             fade = jnp.exp(end_b[pl.ds(h, 1), :] - cum_b[h])
             scaled = (key.astype(F32) * fade).astype(BF16)
             state = lax.dot_general(scaled, value, over_rows, preferred_element_type=F32)
-            s_out[c, i // hc, pl.ds((i % hc) * dim, dim), :] = state.astype(BF16)
-
-        each_head(c, one)
+            s_out[c, peer, u * dim : (u + 1) * dim, :] = state.astype(BF16)
+
         if c == 0:
             pl.semaphore_wait(barrier, group + planes - 2)
+
+        def send(step, peer):
+            @pl.when(step < group)
+            def _():
+                s_copy(c, peer, me).start()
+
+        each_owner(c, 1, nothing, one, send)
+        if c == 0:
             each_peer(lambda peer: end_copy(peer, me).start())
             ends_in[me] = ends[me]
-        each_peer(lambda peer: s_copy(c, peer, me).start())
         s_in[c, me] = s_out[c, me]
 
     def inside(c):
@@ -270,16 +298,21 @@
                 come_x[part, :] = fade * come_x[part, :] + t_in[c, p, part, :].astype(F32)
 
         earlier_planes(add)
-        for i in range(hc):
-            part = pl.ds(i * dim, dim)
-            at = c * hc + i
-            come = come_x[part, :]
-            i_out[c, 0, part, :] = come.astype(BF16)
-            fade = jnp.zeros((1, dim), F32)
-            for j in range(1, group):
-                fade = fade + ends_in[j - 1, at : at + 1, :]
-                i_out[c, j, part, :] = (pre[c, j, part, :] + jnp.exp(fade) * come).astype(BF16)
-        each_peer(lambda peer: i_copy(c, peer, me).start())
+        fades = [jnp.zeros((1, dim), F32)] * hc
+        for j in range(group):
+            for i in range(hc):
+                part = pl.ds(i * dim, dim)
+                at = c * hc + i
+                come = come_x[part, :]
+                if j > 0:
+                    fades[i] = fades[i] + ends_in[j - 1, at : at + 1, :]
+                    come = pre[c, j, part, :] + jnp.exp(fades[i]) * come
+                i_out[c, j, part, :] = come.astype(BF16)
+
+            @pl.when(j != me)
+            def _():
+                i_copy(c, j, me).start()
+
         i_in[c, me] = i_out[c, me]
 
     def give(c):
@@ -288,16 +321,18 @@
         )
 
     def finish(c):
-        each_peer(lambda peer: i_copy(c, peer, peer).wait_recv())
-
-        def one(i, h):
-            come = i_in[c, i // hc, pl.ds((i % hc) * dim, dim), :]
+        def arrive(step, peer):
+            @pl.when(step > 0)
+            def _():
+                i_copy(c, peer, peer).wait_recv()
+
+        def one(i, h, peer, u):
+            come = i_in[c, peer, u * dim : (u + 1) * dim, :]
             inter = jnp.dot(q_hm[h], come, preferred_element_type=F32)
-            mixed = (intra[h] + inter * jnp.exp(cum_b[h])).astype(BF16).astype(F32)
-            squares[...] += mixed * mixed
+            mixed = intra[h] + inter * jnp.exp(cum_b[h])
             tmp_a[pl.ds(i, rows, stride=width), :] = mixed
 
-        each_head(c, one)
+        each_owner(c, 0, arrive, one, nothing)
 
         def some_rows(b, carry):
             span = step_rows * width
@@ -319,8 +354,6 @@
     spread_out(chunks - 1)
     for c in range(chunks):
         finish(c)
-    meansq = jnp.sum(squares[...], axis=1, keepdims=True) * (1.0 / (heads * dim))
-    scale_ref[...] = jnp.broadcast_to(lax.rsqrt(meansq + 1e-06), scale_ref.shape)
 
     each_peer(lambda peer: end_copy(peer, me).wait_send())
     later_planes(lambda step: d_copy(step, plane).wait_send())
@@ -331,8 +364,24 @@
         give(c).wait()
 
 
-def normalize(mixed, scale, out_gain):
-    return (mixed.astype(F32) * scale[:, None, :] * out_gain[None]).astype(BF16)
+def norm_kernel(mixed_ref, gain_ref, out_ref):
+    values = mixed_ref[...].astype(F32)
+    squares = jnp.sum(jnp.sum(values * values, axis=1, keepdims=True), axis=2, keepdims=True)
+    meansq = squares * (1.0 / (values.shape[1] * values.shape[2]))
+    out_ref[...] = (values * lax.rsqrt(meansq + 1e-06) * gain_ref[...][None]).astype(BF16)
+
+
+def normalize(mixed, out_gain):
+    rows, heads, dim = mixed.shape
+    block = 32 if rows % 32 == 0 else 16
+    spec = pl.BlockSpec((block, heads, dim), lambda i: (i, 0, 0))
+    return pl.pallas_call(
+        norm_kernel,
+        out_shape=jax.ShapeDtypeStruct(mixed.shape, BF16),
+        grid=(rows // block,),
+        in_specs=[spec, pl.BlockSpec((heads, dim), lambda i: (0, 0))],
+        out_specs=spec,
+    )(mixed, out_gain)
 
 
 def shards(n_ctx, n_head, queries, keys, values, decay_log, out_gain):
@@ -345,14 +394,11 @@
     dma = pltpu.SemaphoreType.DMA
     planes = n_ctx // inner
     tile = (max(8, per_owner), dim)
-    mixed, scale = pl.pallas_call(
+    mixed = pl.pallas_call(
         functools.partial(kernel, n_ctx, n_head),
-        out_shape=(
-            jax.ShapeDtypeStruct((rows, heads, dim), BF16),
-            jax.ShapeDtypeStruct((rows, dim), F32),
-        ),
+        out_shape=jax.ShapeDtypeStruct((rows, heads, dim), BF16),
         in_specs=[pl.BlockSpec(memory_space=pl.ANY)] * 3 + [pl.BlockSpec(memory_space=pltpu.VMEM)],
-        out_specs=(pl.BlockSpec(memory_space=pl.ANY), pl.BlockSpec(memory_space=pltpu.VMEM)),
+        out_specs=pl.BlockSpec(memory_space=pl.ANY),
         scratch_shapes=[
             held, held, held,
             pltpu.VMEM((rows * width, dim), F32), pltpu.VMEM((rows * width, dim), F32),
@@ -368,7 +414,6 @@
             pltpu.VMEM((chunks,) + block, BF16), pltpu.VMEM((chunks, planes) + block, BF16),
             pltpu.VMEM(block, F32),
             pltpu.VMEM((chunks, group) + block, BF16), pltpu.VMEM((chunks, group) + block, BF16),
-            pltpu.VMEM((rows, dim), F32),
             dma((3, chunks)),
             dma((group,)), dma((group,)),
             dma((chunks, group)), dma((chunks, group)),
@@ -386,7 +431,7 @@
             transcendentals=0,
         ),
     )(queries, keys, values, decay_log.T)
-    return normalize(mixed, scale, out_gain)
+    return normalize(mixed, out_gain)
 
 
 def solution(mesh):

time: 63.2 us -> 63.9 us (1.011)
  Pallas kernels: 58.1 us -> 63.6 us
  other arithmetic: 4.58 us -> 0 us
    pallas_call x1 -> x2, Pallas kernels: 58.1 us -> 63.6 us  [the longest x1 57.8 us: shards(): pl.pallas_call(functools.partial(kernel, n_ctx, n_head), out_shape=jax.Sh...]
    convert_element_type x1 -> x0, other arithmetic: 4.58 us -> none  [normalize(): return (mixed.astype(F32) * scale[:, None, :] * out_gain[None]).astype(BF16)]
where the time goes in v3:
time: 63.9 us; the launch traced here: 63.6 us
  Pallas kernels  63.6 us (100%)
    pallas_call x1, Pallas kernels, shards(): pl.pallas_call(functools.partial(kernel, n_ctx, n_head), out_shape=jax.Sh...  57.8 us
    pallas_call x1, Pallas kernels, normalize(): pl.pallas_call(norm_kernel, out_shape=jax.ShapeDtypeStruct(mixed.shape, B...  5.87 us

profile of v3, /device:TPU:1, one launch (start us, length us, event | category | flops | bytes accessed | tf_op | source)
XLA Modules:
  0.0 63.6 jit_solution(3295945084752260210)
XLA Ops:
  0.0 57.8 %shard_map.55.mixed_ref = bf16[192,64,128]{2,1,0:T(8,128)(2,1)} custom-call(bf16[192,64,128]{2,1,0:T(8,128)(2,1)} %q_hbm.1, bf16[192,64,128]{2,1,0:T(8,128)(2,1)} %k_hbm.1, bf16[192,64,128]{2,1,0:T(8,128)(2,1)} %v_hbm.1, bf16[64,192]{1,0:T(8,128)(2,1)} %bitcast.1), custom_call_target="tpu_custom_call" | custom-call | flops 1610612736 | bytes 12582912 | tf_op jit(solution)/shard_map/pallas_call | solution.py:397
  57.8 5.9 %shard_map.56 = bf16[192,64,128]{2,1,0:T(8,128)(2,1)} custom-call(bf16[192,64,128]{2,1,0:T(8,128)(2,1)} %shard_map.55.mixed_ref, f32[64,128]{1,0:T(8,128)} %gain_ref.1), custom_call_target="tpu_custom_call" | custom-call | tf_op jit(solution)/shard_map/pallas_call | solution.py:378

commit v4 on v3

--- a/solution.py
+++ b/solution.py
@@ -32,10 +32,10 @@
 
 
 def kernel(
-    n_ctx, n_head, q_hbm, k_hbm, v_hbm, dec_ref, mix_hbm,
+    n_ctx, n_head, q_hbm, k_hbm, v_hbm, dec_ref, mix_ref, scale_ref,
     q_in, k_in, v_in, tmp_a, tmp_b, q_hm, k_hm, v_hm, cum_b, cum_t, end_b, intra,
-    ends, ends_in, s_out, s_in, pre, tot_out, tot_in, t_out, t_in, come_x, i_out, i_in,
-    in_sem, e_send, e_recv, s_send, s_recv, d_send, d_recv, t_send, t_recv, i_send, i_recv, o_sem,
+    ends, ends_in, s_out, s_in, pre, tot_out, tot_in, t_out, t_in, come_x, i_out, i_in, squares,
+    in_sem, e_send, e_recv, s_send, s_recv, d_send, d_recv, t_send, t_recv, i_send, i_recv,
 ):
     rows, heads, dim = q_hbm.shape
     inner, group, per_owner, chunks = plan(n_ctx, n_head, heads)
@@ -90,6 +90,7 @@
         for c in range(chunks):
             at = c * width + o * hc
             ends[o, c * hc : (c + 1) * hc, :] = end_b[at : at + hc, :]
+    squares[...] = jnp.zeros_like(squares)
     some = 8
     h_at = lax.broadcasted_iota(jnp.int32, (heads, some * dim), 0)
     l_at = lax.broadcasted_iota(jnp.int32, (heads, some * dim), 1) // dim
@@ -315,11 +316,6 @@
 
         i_in[c, me] = i_out[c, me]
 
-    def give(c):
-        return pltpu.make_async_copy(
-            q_in.at[c], mix_hbm.at[:, pl.ds(c * width, width), :], o_sem.at[c]
-        )
-
     def finish(c):
         def arrive(step, peer):
             @pl.when(step > 0)
@@ -329,20 +325,20 @@
         def one(i, h, peer, u):
             come = i_in[c, peer, u * dim : (u + 1) * dim, :]
             inter = jnp.dot(q_hm[h], come, preferred_element_type=F32)
-            mixed = intra[h] + inter * jnp.exp(cum_b[h])
+            mixed = (intra[h] + inter * jnp.exp(cum_b[h])).astype(BF16).astype(F32)
+            squares[...] += mixed * mixed
             tmp_a[pl.ds(i, rows, stride=width), :] = mixed
 
         each_owner(c, 0, arrive, one, nothing)
 
         def some_rows(b, carry):
             span = step_rows * width
-            q_in[c, pl.ds(b * step_rows, step_rows)] = (
+            mix_ref[pl.ds(b * step_rows, step_rows), c * width : (c + 1) * width, :] = (
                 tmp_a[pl.ds(b * span, span), :].reshape(step_rows, width, dim).astype(BF16)
             )
             return carry
 
         lax.fori_loop(0, rows // step_rows, some_rows, 0)
-        give(c).start()
 
     for c in range(chunks):
         states(c)
@@ -354,6 +350,8 @@
     spread_out(chunks - 1)
     for c in range(chunks):
         finish(c)
+    meansq = jnp.sum(squares[...], axis=1, keepdims=True) * (1.0 / (heads * dim))
+    scale_ref[...] = jnp.broadcast_to(lax.rsqrt(meansq + 1e-06), scale_ref.shape)
 
     each_peer(lambda peer: end_copy(peer, me).wait_send())
     later_planes(lambda step: d_copy(step, plane).wait_send())
@@ -361,27 +359,10 @@
         each_peer(lambda peer: s_copy(c, peer, me).wait_send())
         each_peer(lambda peer: i_copy(c, peer, me).wait_send())
         later_planes(lambda step: t_copy(c, step, plane).wait_send())
-        give(c).wait()
-
-
-def norm_kernel(mixed_ref, gain_ref, out_ref):
-    values = mixed_ref[...].astype(F32)
-    squares = jnp.sum(jnp.sum(values * values, axis=1, keepdims=True), axis=2, keepdims=True)
-    meansq = squares * (1.0 / (values.shape[1] * values.shape[2]))
-    out_ref[...] = (values * lax.rsqrt(meansq + 1e-06) * gain_ref[...][None]).astype(BF16)
-
-
-def normalize(mixed, out_gain):
-    rows, heads, dim = mixed.shape
-    block = 32 if rows % 32 == 0 else 16
-    spec = pl.BlockSpec((block, heads, dim), lambda i: (i, 0, 0))
-    return pl.pallas_call(
-        norm_kernel,
-        out_shape=jax.ShapeDtypeStruct(mixed.shape, BF16),
-        grid=(rows // block,),
-        in_specs=[spec, pl.BlockSpec((heads, dim), lambda i: (0, 0))],
-        out_specs=spec,
-    )(mixed, out_gain)
+
+
+def normalize(mixed, scale, out_gain):
+    return (mixed.astype(F32) * scale[:, None, :] * out_gain[None]).astype(BF16)
 
 
 def shards(n_ctx, n_head, queries, keys, values, decay_log, out_gain):
@@ -394,11 +375,14 @@
     dma = pltpu.SemaphoreType.DMA
     planes = n_ctx // inner
     tile = (max(8, per_owner), dim)
-    mixed = pl.pallas_call(
+    mixed, scale = pl.pallas_call(
         functools.partial(kernel, n_ctx, n_head),
-        out_shape=jax.ShapeDtypeStruct((rows, heads, dim), BF16),
+        out_shape=(
+            jax.ShapeDtypeStruct((rows, heads, dim), BF16),
+            jax.ShapeDtypeStruct((rows, dim), F32),
+        ),
         in_specs=[pl.BlockSpec(memory_space=pl.ANY)] * 3 + [pl.BlockSpec(memory_space=pltpu.VMEM)],
-        out_specs=pl.BlockSpec(memory_space=pl.ANY),
+        out_specs=(pl.BlockSpec(memory_space=pltpu.VMEM),) * 2,
         scratch_shapes=[
             held, held, held,
             pltpu.VMEM((rows * width, dim), F32), pltpu.VMEM((rows * width, dim), F32),
@@ -414,16 +398,16 @@
             pltpu.VMEM((chunks,) + block, BF16), pltpu.VMEM((chunks, planes) + block, BF16),
             pltpu.VMEM(block, F32),
             pltpu.VMEM((chunks, group) + block, BF16), pltpu.VMEM((chunks, group) + block, BF16),
+            pltpu.VMEM((rows, dim), F32),
             dma((3, chunks)),
             dma((group,)), dma((group,)),
             dma((chunks, group)), dma((chunks, group)),
             dma((planes,)), dma((planes,)),
             dma((chunks, planes)), dma((chunks, planes)),
             dma((chunks, group)), dma((chunks, group)),
-            dma((chunks,)),
         ],
         compiler_params=pltpu.CompilerParams(
-            collective_id=0, has_side_effects=True, vmem_limit_bytes=60 * 2**20
+            collective_id=0, has_side_effects=True, vmem_limit_bytes=50 * 2**20
         ),
         cost_estimate=pl.CostEstimate(
             flops=8 * rows * heads * dim * dim,
@@ -431,7 +415,7 @@
             transcendentals=0,
         ),
     )(queries, keys, values, decay_log.T)
-    return normalize(mixed, out_gain)
+    return normalize(mixed, scale, out_gain)
 
 
 def solution(mesh):

time: 63.9 us -> 60.8 us (0.951)
  Pallas kernels: 63.6 us -> 57.1 us
  other arithmetic: 0 us -> 2.71 us
  local copies, waits for them, and re-layouts: 0 us -> 0.76 us
    pallas_call x2 -> x1, Pallas kernels: 63.6 us -> 57.1 us  [shards(): pl.pallas_call(functools.partial(kernel, n_ctx, n_head), out_shape=(jax.S...]
    convert_element_type x0 -> x1, other arithmetic: none -> 2.71 us  [normalize(): return (mixed.astype(F32) * scale[:, None, :] * out_gain[None]).astype(BF16)]
    unnamed x0 -> x4, local copies, waits for them, and re-layouts: none -> 0.76 us
where the time goes in v4:
time: 60.8 us; the launch traced here: 60.6 us
  Pallas kernels  57.1 us (94%)
  other arithmetic  2.71 us (4%)
  local copies, waits for them, and re-layouts  0.76 us (1%)
    pallas_call x1, Pallas kernels, shards(): pl.pallas_call(functools.partial(kernel, n_ctx, n_head), out_shape=(jax.S...  57.1 us
    convert_element_type x1, other arithmetic, normalize(): return (mixed.astype(F32) * scale[:, None, :] * out_gain[None]).astype(BF16)  2.71 us

profile of v4, /device:TPU:1, one launch (start us, length us, event | category | flops | bytes accessed | tf_op | source)
XLA Modules:
  0.0 60.6 jit_solution(8790764017680896036)
XLA Ops:
  0.0 0.0 copy-start
  0.0 0.8 %copy-done = bf16[192,64]{0,1:T(8,128)(2,1)S(1)} copy-done((bf16[192,64]{0,1:T(8,128)(2,1)S(1)}, bf16[192,64]{0,1:T(8,128)(2,1)}, u32[]{:S(2)}) %copy-start) | copy-done | bytes 24600
  0.8 0.0 copy-start.1
  0.8 57.1 %shard_map.55 = (bf16[192,64,128]{2,1,0:T(8,128)(2,1)S(1)}, f32[192,128]{1,0:T(8,128)S(1)}) custom-call(bf16[192,64,128]{2,1,0:T(8,128)(2,1)} %q_hbm.1, bf16[192,64,128]{2,1,0:T(8,128)(2,1)} %k_hbm.1, bf16[192,64,128]{2,1,0:T(8,128)(2,1)} %v_hbm.1, bf16[64,192]{1,0:T(8,128)(2,1)S(1)} %bitcast.1), custom_call_target="tpu_custom_call" | custom-call | flops 1610612736 | bytes 12582912 | tf_op jit(solution)/shard_map/pallas_call | solution.py:378
  57.9 0.0 copy-done.1
  57.9 2.7 %multiply_convert_fusion = bf16[192,64,128]{2,1,0:T(8,128)(2,1)} fusion(bf16[192,64,128]{2,1,0:T(8,128)(2,1)S(1)} %get-tuple-element.7, f32[64,128]{1,0:T(8,128)S(1)} %copy-done.1, f32[192,128]{1,0:T(8,128)S(1)} %get-tuple-element.8), kind=kLoop, calls=%fused_computation | loop fusion | flops 6291456 | bytes 6422528 | tf_op jit(solution)/shard_map/convert_element_type | solution.py:365
Async XLA Ops:
  0.0 0.8 %copy-start = (bf16[192,64]{0,1:T(8,128)(2,1)S(1)}, bf16[192,64]{0,1:T(8,128)(2,1)}, u32[]{:S(2)}) copy-start(bf16[192,64]{0,1:T(8,128)(2,1)} %param.8) | copy-start | bytes 73732
  0.8 57.1 %copy-start.1 = (f32[64,128]{1,0:T(8,128)S(1)}, f32[64,128]{1,0:T(8,128)}, u32[]{:S(2)}) copy-start(f32[64,128]{1,0:T(8,128)} %param.9) | copy-start | bytes 98308

commit v5 on v4

--- a/solution.py
+++ b/solution.py
@@ -157,13 +157,14 @@
                 body(p)
 
     step_rows = 16
+    pitch = width + 1
 
     def activate(held, c, tmp):
         def some_rows(b, carry):
-            x = held[c, pl.ds(b * step_rows, step_rows)].astype(F32)
-            tmp[pl.ds(b * step_rows * width, step_rows * width), :] = silu(x).reshape(
-                step_rows * width, dim
-            )
+            x = silu(held[c, pl.ds(b * step_rows, step_rows)].astype(F32))
+            base = pl.multiple_of(b * (step_rows * pitch), step_rows)
+            for t in range(step_rows):
+                tmp[pl.ds(base + t * pitch, width), :] = x[t]
             return carry
 
         lax.fori_loop(0, rows // step_rows, some_rows, 0)
@@ -213,8 +214,8 @@
         activate(v_in, c, tmp_b)
 
         def one(i, h, peer, u):
-            key = tmp_a[pl.ds(i, rows, stride=width), :].astype(BF16)
-            value = tmp_b[pl.ds(i, rows, stride=width), :].astype(BF16)
+            key = tmp_a[pl.ds(i, rows, stride=pitch), :].astype(BF16)
+            value = tmp_b[pl.ds(i, rows, stride=pitch), :].astype(BF16)
             k_hm[h] = key
             v_hm[h] = value
             fade = jnp.exp(end_b[pl.ds(h, 1), :] - cum_b[h])
@@ -241,7 +242,7 @@
         activate(q_in, c, tmp_a)
 
         def one(i, h):
-            query = tmp_a[pl.ds(i, rows, stride=width), :].astype(BF16)
+            query = tmp_a[pl.ds(i, rows, stride=pitch), :].astype(BF16)
             q_hm[h] = query
             key, value, cum = k_hm[h], v_hm[h], cum_b[h]
             row = cum_t[pl.ds(h, 1), :]
@@ -327,15 +328,16 @@
             inter = jnp.dot(q_hm[h], come, preferred_element_type=F32)
             mixed = (intra[h] + inter * jnp.exp(cum_b[h])).astype(BF16).astype(F32)
             squares[...] += mixed * mixed
-            tmp_a[pl.ds(i, rows, stride=width), :] = mixed
+            tmp_a[pl.ds(i, rows, stride=pitch), :] = mixed
 
         each_owner(c, 0, arrive, one, nothing)
 
         def some_rows(b, carry):
-            span = step_rows * width
-            mix_ref[pl.ds(b * step_rows, step_rows), c * width : (c + 1) * width, :] = (
-                tmp_a[pl.ds(b * span, span), :].reshape(step_rows, width, dim).astype(BF16)
-            )
+            base = pl.multiple_of(b * (step_rows * pitch), step_rows)
+            for t in range(step_rows):
+                mix_ref[b * step_rows + t, c * width : (c + 1) * width, :] = tmp_a[
+                    pl.ds(base + t * pitch, width), :
+                ].astype(BF16)
             return carry
 
         lax.fori_loop(0, rows // step_rows, some_rows, 0)
@@ -385,7 +387,7 @@
         out_specs=(pl.BlockSpec(memory_space=pltpu.VMEM),) * 2,
         scratch_shapes=[
             held, held, held,
-            pltpu.VMEM((rows * width, dim), F32), pltpu.VMEM((rows * width, dim), F32),
+            pltpu.VMEM((rows * (width + 1), dim), F32), pltpu.VMEM((rows * (width + 1), dim), F32),
             major, major, major,
             pltpu.VMEM((heads, rows, dim), F32),
             pltpu.VMEM((heads, rows), F32),

time: 60.8 us -> 60 us (0.987)
  Pallas kernels: 57.1 us -> 56.3 us
    pallas_call x1, Pallas kernels: 57.1 us -> 56.3 us  [shards(): pl.pallas_call(functools.partial(kernel, n_ctx, n_head), out_shape=(jax.S...]
where the time goes in v5:
time: 60 us; the launch traced here: 59.8 us
  Pallas kernels  56.3 us (94%)
  other arithmetic  2.71 us (5%)
  local copies, waits for them, and re-layouts  0.76 us (1%)
    pallas_call x1, Pallas kernels, shards(): pl.pallas_call(functools.partial(kernel, n_ctx, n_head), out_shape=(jax.S...  56.3 us
    convert_element_type x1, other arithmetic, normalize(): return (mixed.astype(F32) * scale[:, None, :] * out_gain[None]).astype(BF16)  2.71 us

profile of v5, /device:TPU:1, one launch (start us, length us, event | category | flops | bytes accessed | tf_op | source)
XLA Modules:
  0.0 59.8 jit_solution(2981743908928200969)
XLA Ops:
  0.0 0.0 copy-start
  0.0 0.8 %copy-done = bf16[192,64]{0,1:T(8,128)(2,1)S(1)} copy-done((bf16[192,64]{0,1:T(8,128)(2,1)S(1)}, bf16[192,64]{0,1:T(8,128)(2,1)}, u32[]{:S(2)}) %copy-start) | copy-done | bytes 24600
  0.8 0.0 copy-start.1
  0.8 56.3 %shard_map.55 = (bf16[192,64,128]{2,1,0:T(8,128)(2,1)S(1)}, f32[192,128]{1,0:T(8,128)S(1)}) custom-call(bf16[192,64,128]{2,1,0:T(8,128)(2,1)} %q_hbm.1, bf16[192,64,128]{2,1,0:T(8,128)(2,1)} %k_hbm.1, bf16[192,64,128]{2,1,0:T(8,128)(2,1)} %v_hbm.1, bf16[64,192]{1,0:T(8,128)(2,1)S(1)} %bitcast.1), custom_call_target="tpu_custom_call" | custom-call | flops 1610612736 | bytes 12582912 | tf_op jit(solution)/shard_map/pallas_call | solution.py:380
  57.1 0.0 copy-done.1
  57.1 2.7 %multiply_convert_fusion = bf16[192,64,128]{2,1,0:T(8,128)(2,1)} fusion(bf16[192,64,128]{2,1,0:T(8,128)(2,1)S(1)} %get-tuple-element.7, f32[64,128]{1,0:T(8,128)S(1)} %copy-done.1, f32[192,128]{1,0:T(8,128)S(1)} %get-tuple-element.8), kind=kLoop, calls=%fused_computation | loop fusion | flops 6291456 | bytes 6422528 | tf_op jit(solution)/shard_map/convert_element_type | solution.py:367
Async XLA Ops:
  0.0 0.8 %copy-start = (bf16[192,64]{0,1:T(8,128)(2,1)S(1)}, bf16[192,64]{0,1:T(8,128)(2,1)}, u32[]{:S(2)}) copy-start(bf16[192,64]{0,1:T(8,128)(2,1)} %param.8) | copy-start | bytes 73732
  0.8 56.3 %copy-start.1 = (f32[64,128]{1,0:T(8,128)S(1)}, f32[64,128]{1,0:T(8,128)}, u32[]{:S(2)}) copy-start(f32[64,128]{1,0:T(8,128)} %param.9) | copy-start | bytes 98308

commit v6 on v5

--- a/solution.py
+++ b/solution.py
@@ -86,10 +86,6 @@
     over_rows = (((0,), (0,)), ((), ()))
     cum_t[...] = jnp.dot(decays, upper, preferred_element_type=F32)
     end_b[...] = jnp.dot(decays, jnp.ones((rows, dim), BF16), preferred_element_type=F32)
-    for o in range(group):
-        for c in range(chunks):
-            at = c * width + o * hc
-            ends[o, c * hc : (c + 1) * hc, :] = end_b[at : at + hc, :]
     squares[...] = jnp.zeros_like(squares)
     some = 8
     h_at = lax.broadcasted_iota(jnp.int32, (heads, some * dim), 0)
@@ -169,7 +165,7 @@
 
         lax.fori_loop(0, rows // step_rows, some_rows, 0)
 
-    unroll = 4
+    unroll = 8
 
     def each_head(c, body):
         def one(g, carry):
@@ -233,6 +229,10 @@
 
         each_owner(c, 1, nothing, one, send)
         if c == 0:
+            for o in range(group):
+                for d in range(chunks):
+                    at = d * width + o * hc
+                    ends[o, d * hc : (d + 1) * hc, :] = end_b[at : at + hc, :]
             each_peer(lambda peer: end_copy(peer, me).start())
             ends_in[me] = ends[me]
         s_in[c, me] = s_out[c, me]
@@ -255,9 +255,12 @@
                     preferred_element_type=F32,
                 )
                 offset = cum[s0:, :w] - row[:, s0 : s0 + w]
-                tt = lax.broadcasted_iota(jnp.int32, (n, w), 0)
-                ss = lax.broadcasted_iota(jnp.int32, (n, w), 1)
-                weights = scores * jnp.exp(jnp.where(ss <= tt, offset, -1e30))
+                tt = lax.broadcasted_iota(jnp.int32, (w, w), 0)
+                ss = lax.broadcasted_iota(jnp.int32, (w, w), 1)
+                fades = jnp.exp(jnp.where(ss <= tt, offset[:w], -1e30))
+                if n > w:
+                    fades = jnp.concatenate([fades, jnp.exp(offset[w:])], axis=0)
+                weights = scores * fades
                 outs.append(
                     jnp.dot(
                         weights.astype(BF16), value[s0 : s0 + w], preferred_element_type=F32

time: 60 us -> 59.6 us (level)
  no operation moved by 1% of the time
where the time goes in v6:
time: 59.6 us; the launch traced here: 59.4 us
  Pallas kernels  55.9 us (94%)
  other arithmetic  2.71 us (5%)
  local copies, waits for them, and re-layouts  0.76 us (1%)
    pallas_call x1, Pallas kernels, shards(): pl.pallas_call(functools.partial(kernel, n_ctx, n_head), out_shape=(jax.S...  55.9 us
    convert_element_type x1, other arithmetic, normalize(): return (mixed.astype(F32) * scale[:, None, :] * out_gain[None]).astype(BF16)  2.71 us

profile of v6, /device:TPU:1, one launch (start us, length us, event | category | flops | bytes accessed | tf_op | source)
XLA Modules:
  0.0 59.4 jit_solution(8388730098091089326)
XLA Ops:
  0.0 0.0 copy-start
  0.0 0.8 %copy-done = bf16[192,64]{0,1:T(8,128)(2,1)S(1)} copy-done((bf16[192,64]{0,1:T(8,128)(2,1)S(1)}, bf16[192,64]{0,1:T(8,128)(2,1)}, u32[]{:S(2)}) %copy-start) | copy-done | bytes 24600
  0.8 0.0 copy-start.1
  0.8 55.9 %shard_map.55 = (bf16[192,64,128]{2,1,0:T(8,128)(2,1)S(1)}, f32[192,128]{1,0:T(8,128)S(1)}) custom-call(bf16[192,64,128]{2,1,0:T(8,128)(2,1)} %q_hbm.1, bf16[192,64,128]{2,1,0:T(8,128)(2,1)} %k_hbm.1, bf16[192,64,128]{2,1,0:T(8,128)(2,1)} %v_hbm.1, bf16[64,192]{1,0:T(8,128)(2,1)S(1)} %bitcast.1), custom_call_target="tpu_custom_call" | custom-call | flops 1610612736 | bytes 12582912 | tf_op jit(solution)/shard_map/pallas_call | solution.py:383
  56.7 0.0 copy-done.1
  56.7 2.7 %multiply_convert_fusion = bf16[192,64,128]{2,1,0:T(8,128)(2,1)} fusion(bf16[192,64,128]{2,1,0:T(8,128)(2,1)S(1)} %get-tuple-element.7, f32[64,128]{1,0:T(8,128)S(1)} %copy-done.1, f32[192,128]{1,0:T(8,128)S(1)} %get-tuple-element.8), kind=kLoop, calls=%fused_computation | loop fusion | flops 6291456 | bytes 6422528 | tf_op jit(solution)/shard_map/convert_element_type | solution.py:370
Async XLA Ops:
  0.0 0.8 %copy-start = (bf16[192,64]{0,1:T(8,128)(2,1)S(1)}, bf16[192,64]{0,1:T(8,128)(2,1)}, u32[]{:S(2)}) copy-start(bf16[192,64]{0,1:T(8,128)(2,1)} %param.8) | copy-start | bytes 73732
  0.8 55.9 %copy-start.1 = (f32[64,128]{1,0:T(8,128)S(1)}, f32[64,128]{1,0:T(8,128)}, u32[]{:S(2)}) copy-start(f32[64,128]{1,0:T(8,128)} %param.9) | copy-start | bytes 98308

commit v7 on v6

--- a/solution.py
+++ b/solution.py
@@ -345,14 +345,18 @@
 
         lax.fori_loop(0, rows // step_rows, some_rows, 0)
 
+    ahead = 2
     for c in range(chunks):
         states(c)
+        if c >= ahead:
+            join(c - ahead)
+    for c in range(max(chunks - ahead, 0), min(ahead, chunks)):
+        join(c)
     for c in range(chunks):
-        join(c)
+        spread_out(c)
         inside(c)
-        if c > 0:
-            spread_out(c - 1)
-    spread_out(chunks - 1)
+        if c + ahead < chunks:
+            join(c + ahead)
     for c in range(chunks):
         finish(c)
     meansq = jnp.sum(squares[...], axis=1, keepdims=True) * (1.0 / (heads * dim))

time: 59.6 us -> 59.6 us (level)
  no operation moved by 1% of the time
where the time goes in v7:
time: 59.6 us; the launch traced here: 59.4 us
  Pallas kernels  55.9 us (94%)
  other arithmetic  2.71 us (5%)
  local copies, waits for them, and re-layouts  0.76 us (1%)
    pallas_call x1, Pallas kernels, shards(): pl.pallas_call(functools.partial(kernel, n_ctx, n_head), out_shape=(jax.S...  55.9 us
    convert_element_type x1, other arithmetic, normalize(): return (mixed.astype(F32) * scale[:, None, :] * out_gain[None]).astype(BF16)  2.71 us

profile of v7, /device:TPU:1, one launch (start us, length us, event | category | flops | bytes accessed | tf_op | source)
XLA Modules:
  0.0 59.4 jit_solution(12296236816276940131)
XLA Ops:
  0.0 0.0 copy-start
  0.0 0.8 %copy-done = bf16[192,64]{0,1:T(8,128)(2,1)S(1)} copy-done((bf16[192,64]{0,1:T(8,128)(2,1)S(1)}, bf16[192,64]{0,1:T(8,128)(2,1)}, u32[]{:S(2)}) %copy-start) | copy-done | bytes 24600
  0.8 0.0 copy-start.1
  0.8 55.9 %shard_map.55 = (bf16[192,64,128]{2,1,0:T(8,128)(2,1)S(1)}, f32[192,128]{1,0:T(8,128)S(1)}) custom-call(bf16[192,64,128]{2,1,0:T(8,128)(2,1)} %q_hbm.1, bf16[192,64,128]{2,1,0:T(8,128)(2,1)} %k_hbm.1, bf16[192,64,128]{2,1,0:T(8,128)(2,1)} %v_hbm.1, bf16[64,192]{1,0:T(8,128)(2,1)S(1)} %bitcast.1), custom_call_target="tpu_custom_call" | custom-call | flops 1610612736 | bytes 12582912 | tf_op jit(solution)/shard_map/pallas_call | solution.py:387
  56.7 0.0 copy-done.1
  56.7 2.7 %multiply_convert_fusion = bf16[192,64,128]{2,1,0:T(8,128)(2,1)} fusion(bf16[192,64,128]{2,1,0:T(8,128)(2,1)S(1)} %get-tuple-element.7, f32[64,128]{1,0:T(8,128)S(1)} %copy-done.1, f32[192,128]{1,0:T(8,128)S(1)} %get-tuple-element.8), kind=kLoop, calls=%fused_computation | loop fusion | flops 6291456 | bytes 6422528 | tf_op jit(solution)/shard_map/convert_element_type | solution.py:374
Async XLA Ops:
  0.0 0.8 %copy-start = (bf16[192,64]{0,1:T(8,128)(2,1)S(1)}, bf16[192,64]{0,1:T(8,128)(2,1)}, u32[]{:S(2)}) copy-start(bf16[192,64]{0,1:T(8,128)(2,1)} %param.8) | copy-start | bytes 73732
  0.8 55.9 %copy-start.1 = (f32[64,128]{1,0:T(8,128)S(1)}, f32[64,128]{1,0:T(8,128)}, u32[]{:S(2)}) copy-start(f32[64,128]{1,0:T(8,128)} %param.9) | copy-start | bytes 98308
